TPU v7x, 512 devices: a whole 4x4x16 slice. The times are simulated.
512 devices in a mesh: space: 128 (over z, y, core), code: 4 (over x).
Axes of the slice: x: 4, y: 4, z: 16, core: 2. Of those that a mesh axis runs over, the one named last changes fastest.
Arguments:
- geometry: bfloat16 [4, 6, 1048576], P('code', None, 'space'), as said below
- codebook: bfloat16 [48, 4096], P(None, 'code'), may hold values from -3 to 3
- word_ids: int32 [1048576], P('space'), may hold values from 0 to 4095
- residual: bfloat16 [12, 1048576], P(None, 'space'), may hold values from -2 to 2
- send_list: int32 [4, 128, 128], P('code', 'space'), may hold values from 0 to 63
- tile_list: int32 [4, 1024, 4], P('code', 'space'), may hold values from 0 to 127, as said below
- rays: float32 [4, 3, 262144], P('code', None, 'space'), as said below
- target: int32 [4, 3, 262144], P('code', None, 'space'), may hold values from 0 to 255
Outputs:
- rendered: float32 [4, 3, 262144], P('code', None, 'space')
- foot_grad: float32 [4, 6, 1048576], P('code', None, 'space')
- resid_grad: float32 [12, 1048576], P(None, 'space')
- code_grad: float32 [48, 4096], P(None, 'code')
Inputs may be any that keep to these rules, and one draw needn't show every extreme that they name: `tile_list`: each row names 4 different owners. `geometry`: conics are positive definite, |b| at most 0.6 sqrt(a c); opacities are positive and at most 0.5. `rays`: every ray has length 0.8 to 1.2; directions may point anywhere.
All inputs are finite; a program needn't handle non-finite values.
Results may differ from a plain program's by a relative error of at most 0.0021.
Values may be sent and summed in bfloat16 or wider, within the bound.
A program may use at most 64 MiB of HBM per device.

v0:
```python
import math
import jax
import jax.numpy as jnp
from jax import lax
from jax.sharding import PartitionSpec as P

WORDS = 4096
COEF = 48
RESID = 12
GEO = 6
BLOCK = 128
LIST = 4
SIDE = 16
TILE_PIX = 256
band_zero = 0.28209479177387814
band_one = 0.4886025119029199
band_two = (
    1.0925484305920792,
    -1.0925484305920792,
    0.31539156525252005,
    -1.0925484305920792,
    0.5462742152960396,
)
band_three = (
    -0.5900435899266435,
    2.890611442640554,
    -0.4570457994644658,
    0.3731763325901154,
    -0.4570457994644658,
    1.445305721320277,
    -0.5900435899266435,
)


def harmonics(direction):
    length = jnp.sqrt(jnp.sum(direction * direction, axis=0))
    coord_x = direction[0] / length
    coord_y = direction[1] / length
    coord_z = direction[2] / length
    square_x = coord_x * coord_x
    square_y = coord_y * coord_y
    square_z = coord_z * coord_z
    entries = [
        band_zero * jnp.ones_like(coord_x),
        -band_one * coord_y,
        band_one * coord_z,
        -band_one * coord_x,
        band_two[0] * coord_x * coord_y,
        band_two[1] * coord_y * coord_z,
        band_two[2] * (2.0 * square_z - square_x - square_y),
        band_two[3] * coord_x * coord_z,
        band_two[4] * (square_x - square_y),
        band_three[0] * coord_y * (3.0 * square_x - square_y),
        band_three[1] * coord_x * coord_y * coord_z,
        band_three[2] * coord_y * (4.0 * square_z - square_x - square_y),
        band_three[3] * coord_z * (2.0 * square_z - 3.0 * square_x - 3.0 * square_y),
        band_three[4] * coord_x * (4.0 * square_z - square_x - square_y),
        band_three[5] * coord_z * (square_x - square_y),
        band_three[6] * coord_x * (square_x - 3.0 * square_y),
    ]
    return jnp.stack(entries)


def pixel_offsets(side):
    pixel_index = jnp.arange(side * side, dtype=jnp.int32)
    offset_u = (pixel_index % side).astype(jnp.float32) - (side - 1) * 0.5
    offset_v = (pixel_index // side).astype(jnp.float32) - (side - 1) * 0.5
    return jnp.stack([offset_u, offset_v])


def composite(footprint, palette, harmonic_rows, offsets):
    delta_u = offsets[0][:, None] - footprint[0][None, :]
    delta_v = offsets[1][:, None] - footprint[1][None, :]
    exponent = -0.5 * (
        footprint[2] * delta_u * delta_u
        + 2.0 * footprint[3] * delta_u * delta_v
        + footprint[4] * delta_v * delta_v
    )
    absorb = footprint[5] * jnp.exp(exponent)
    keep_log = jnp.log1p(-absorb)
    before = jnp.cumsum(keep_log, axis=1) - keep_log
    weight = jnp.exp(before) * absorb
    mixed = jnp.dot(weight, palette.T, precision=lax.Precision.HIGHEST)
    mixed = mixed.reshape(mixed.shape[0], 16, 3)
    return (
        jnp.einsum("kp,pkc->cp", harmonic_rows, mixed, precision=lax.Precision.HIGHEST)
        + 0.5 * jnp.sum(weight, axis=1)[None, :]
    )


def render_group(footprint, palette, harmonic_rows, destination_group, offsets):

    def forward(foot_all, palette_group):
        return jax.vmap(composite, in_axes=(0, 0, 0, None))(
            foot_all, palette_group, harmonic_rows, offsets
        )

    images, pullback = jax.vjp(forward, footprint, palette)
    grad_foot, grad_palette = pullback(images - destination_group)
    return (images, grad_foot, grad_palette)


def decode(codebook, word_ids, residual):
    looked = jnp.take(codebook, word_ids, axis=1).astype(jnp.float32)
    upper = looked[:RESID] + residual.astype(jnp.float32)
    decoded = jnp.concatenate([upper, looked[RESID:]], axis=0).astype(jnp.bfloat16)
    return lax.optimization_barrier(decoded)


def on_device(geometry, codebook, word_ids, residual, send_list, tile_list, rays, target):
    n_space = lax.axis_size("space")
    blocks = word_ids.shape[0] // BLOCK
    tiles_here = tile_list.shape[1]
    list_width = LIST * BLOCK
    full_book = lax.all_gather(codebook, "code", axis=1, tiled=True)
    sent_blocks = send_list[0, 0]
    foot_out = jnp.take(geometry[0].reshape(GEO, blocks, BLOCK), sent_blocks, axis=1)
    decoded = decode(full_book, word_ids, residual)
    palette_out = jnp.take(decoded.reshape(COEF, blocks, BLOCK), sent_blocks, axis=1)
    foot_in, palette_in = (
        lax.all_to_all(foot_out, "space", split_axis=1, concat_axis=1, tiled=True),
        lax.all_to_all(palette_out, "space", split_axis=1, concat_axis=1, tiled=True),
    )
    tile_rows = tile_list[0]
    flat_rows = tile_rows.reshape(-1)
    foot_tiles = (
        jnp.take(foot_in, flat_rows, axis=1).reshape(GEO, tiles_here, list_width).transpose(1, 0, 2)
    )
    palette_tiles = (
        jnp.take(palette_in, flat_rows, axis=1)
        .reshape(COEF, tiles_here, list_width)
        .transpose(1, 0, 2)
    )
    harmonic_tiles = harmonics(rays[0]).reshape(16, tiles_here, TILE_PIX).transpose(1, 0, 2)
    target_tiles = (
        (target[0].astype(jnp.float32) / 255.0).reshape(3, tiles_here, TILE_PIX).transpose(1, 0, 2)
    )
    per_step = math.gcd(tiles_here, 2)
    step_count = tiles_here // per_step
    offsets = pixel_offsets(SIDE)

    def render_step(inputs):
        foot_group, palette_group, harmonic_group, destination_group = inputs
        return render_group(
            foot_group.astype(jnp.float32),
            palette_group.astype(jnp.float32),
            harmonic_group,
            destination_group,
            offsets,
        )

    images, grad_foot, grad_palette = lax.map(
        render_step,
        (
            foot_tiles.reshape(step_count, per_step, GEO, list_width),
            palette_tiles.reshape(step_count, per_step, COEF, list_width),
            harmonic_tiles.reshape(step_count, per_step, 16, TILE_PIX),
            target_tiles.reshape(step_count, per_step, 3, TILE_PIX),
        ),
    )
    tile_grads = jnp.concatenate(
        [
            grad_foot.reshape(tiles_here, GEO, list_width),
            grad_palette.reshape(tiles_here, COEF, list_width),
        ],
        axis=1,
    )
    tile_grads = tile_grads.reshape(tiles_here, GEO + COEF, LIST, BLOCK)
    slot_hot = (
        tile_rows[:, :, None] == jnp.arange(n_space, dtype=jnp.int32)[None, None, :]
    ).astype(jnp.float32)
    slot_grads = jnp.einsum("tln,tclk->cnk", slot_hot, tile_grads, precision=lax.Precision.HIGHEST)
    sent_hot = (sent_blocks[:, None] == jnp.arange(blocks, dtype=jnp.int32)[None, :]).astype(
        jnp.float32
    )
    returned = lax.all_to_all(slot_grads, "space", split_axis=1, concat_axis=1, tiled=True)
    owned = jnp.einsum("cnk,nb->cbk", returned, sent_hot, precision=lax.Precision.HIGHEST).reshape(
        GEO + COEF, blocks * BLOCK
    )
    palette_owned = owned[GEO:]
    word_term = jax.ops.segment_sum(palette_owned.T, word_ids, num_segments=WORDS).T
    resid_part = palette_owned[:RESID]
    foot_grad = owned[:GEO]
    resid_grad = lax.psum(resid_part, "code")
    codeword_portion = lax.psum_scatter(word_term, "code", scatter_dimension=1, tiled=True)
    code_grad = lax.psum(codeword_portion, "space")
    rendered = (
        images.reshape(tiles_here, 3, TILE_PIX)
        .transpose(1, 0, 2)
        .reshape(1, 3, tiles_here * TILE_PIX)
    )
    return (rendered, foot_grad[None], resid_grad, code_grad)


def solution(mesh):
    placed = (
        P("code", None, "space"),
        P(None, "code"),
        P("space"),
        P(None, "space"),
        P("code", "space", None),
        P("code", "space", None),
        P("code", None, "space"),
        P("code", None, "space"),
    )
    return jax.shard_map(
        on_device,
        mesh=mesh,
        in_specs=placed,
        out_specs=(
            P("code", None, "space"),
            P("code", None, "space"),
            P(None, "space"),
            P(None, "code"),
        ),
        check_vma=False,
    )
```

profile of v0, /device:TPU:8, one launch (start us, length us, event | category | flops | bytes accessed | tf_op | source)
XLA Modules:
  0.0 950.6 jit_solution(1836377726024788179)
XLA Ops:
  7.2 0.7 compare_and_fusion.1
  8.5 0.7 gather_fusion
  9.2 0.9 select_bitcast_fusion.3
  10.2 19.5 %all-to-all-start = ((bf16[6,128,128]{2,0,1:T(8,128)(2,1)}), bf16[6,128,128]{2,0,1:T(8,128)(2,1)S(1)}, u32[]{:S(2)}, u32[]{:S(2)}) async-start(bf16[6,128,128]{2,0,1:T(8,128)(2,1)} %select_bitcast_fusion.3), calls=%async_computation | async-start | bytes 524288 | tf_op jit(solution)/shard_map/all_to_all | solution.py:121
  29.7 0.8 compare_and_fusion
  30.4 1.4 fusion.63
  31.8 1.1 copy.230
  32.9 14.9 %all_gather.3 = bf16[48,4096]{0,1:T(8,128)(2,1)S(1)} all-gather(bf16[48,1024]{0,1:T(8,128)(2,1)S(1)} %copy.230), channel_id=1, replica_groups=mesh['space'=128,'code'=4] {'code'}, dimensions={1}, use_global_device_ids=true | all-gather | bytes 491520 | tf_op jit(solution)/shard_map/all_gather | solution.py:115
  47.8 27.9 %gather_fusion.2 = bf16[8192,48]{1,0:T(8,128)(2,1)S(1)} fusion(bf16[48,4096]{0,1:T(8,128)(2,1)S(1)} %all_gather.3, s32[8192]{0:T(1024)} %fusion.63), kind=kCustom, calls=%fused_computation.2 | custom fusion | bytes 1605632 | tf_op jit(solution)/shard_map/jit(_take)/gather | solution.py:104
  75.7 0.8 copy.231
  77.9 0.9 gather_fusion.3
  78.8 1.4 select_bitcast_fusion
  80.2 16.2 %all-to-all-start.1 = ((bf16[48,128,128]{2,0,1:T(8,128)(2,1)}), bf16[48,128,128]{2,0,1:T(8,128)(2,1)S(1)}, u32[]{:S(2)}, u32[]{:S(2)}) async-start(bf16[48,128,128]{2,0,1:T(8,128)(2,1)} %select_bitcast_fusion), calls=%async_computation.1 | async-start | bytes 3145728 | tf_op jit(solution)/shard_map/all_to_all | solution.py:122
  98.1 1.5 gather_fusion.1
  99.7 71.7 %all-to-all-done.1 = bf16[48,128,128]{2,0,1:T(8,128)(2,1)S(1)} async-done(((bf16[48,128,128]{2,0,1:T(8,128)(2,1)}), bf16[48,128,128]{2,0,1:T(8,128)(2,1)S(1)}, u32[]{:S(2)}, u32[]{:S(2)}) %all-to-all-start.1) | async-done | bytes 1572896 | tf_op jit(solution)/shard_map/all_to_all | solution.py:122
  172.5 0.9 copy.256
  173.4 107.2 %while.16 = (s32[]{:T(128)}, f32[4,2,3,256]{3,1,0,2:T(2,128)S(1)}, f32[4,2,6,512]{3,2,1,0:T(8,128)}, f32[4,2,48,512]{3,2,1,0:T(8,128)}, bf16[4,2,6,512]{3,1,0,2:...) while((s32[]{:T(128)}, f32[4,2,3,256]{3,1,0,2:T(2,128)S(1)}, ...), condition=%wide.region_14.15_spmd.clone.clone, body=%wide.region_1.14_spmd.clone.clone.sunk | while | flops 552732160 | bytes 30296212 | solution.py:152
  174.4 1.9 fusion.93
  176.4 2.6 multiply_reduce_fusion.7
  180.0 2.6 fusion.94
  182.7 0.7 fusion.95
  183.5 2.4 fusion.98
  185.9 3.5 multiply_multiply_fusion.3
  190.4 4.3 fusion.96
  195.9 3.5 fusion.97
  201.2 1.9 fusion.93
  203.2 2.6 multiply_reduce_fusion.7
  206.8 2.6 fusion.94
  209.5 0.7 fusion.95
  210.3 2.4 fusion.98
  212.7 3.5 multiply_multiply_fusion.3
  217.1 4.3 fusion.96
  222.7 3.5 fusion.97
  228.0 1.9 fusion.93
  229.9 2.6 multiply_reduce_fusion.7
  233.6 2.6 fusion.94
  236.3 0.7 fusion.95
  237.0 2.4 fusion.98
  239.5 3.5 multiply_multiply_fusion.3
  243.9 4.3 fusion.96
  249.5 3.5 fusion.97
  254.8 1.9 fusion.93
  256.7 2.6 multiply_reduce_fusion.7
  260.3 2.6 fusion.94
  263.1 0.7 fusion.95
  263.8 2.5 fusion.98
  266.3 3.5 multiply_multiply_fusion.3
  270.7 4.3 fusion.96
  276.3 3.5 fusion.97
  280.5 1.4 concatenate.15
  281.9 0.9 reshape.770
  282.9 4.8 convolution_bitcast_fusion.1
  287.6 4.5 copy.243
  292.1 171.6 %all_to_all.15 = f32[54,128,128]{2,0,1:T(8,128)S(1)} all-to-all(f32[54,128,128]{2,0,1:T(8,128)} %copy.243), channel_id=1, replica_groups=mesh['space'=128,'code'=4] {'space'}, dimensions={1} | all-to-all | bytes 7077888 | tf_op jit(solution)/shard_map/all_to_all | solution.py:176
  463.8 1.7 fusion.53
  465.7 2.7 copy.258
  468.4 45.7 %scatter_custom_fusion = f32[4096,48]{1,0:T(8,128)} fusion(s32[8192]{0:T(1024)} %param.12, f32[8192,48]{1,0:T(8,128)} %bitcast.185, f32[]{:T(128)} %constant.114.clone.1), kind=kCustom, calls=%fused_computation.109 | custom fusion | flops 393216 | bytes 786944 | tf_op jit(solution)/shard_map/scatter-add | solution.py:181
  514.1 35.1 %reduce-scatter.2.cloned.1.call-done = f32[48,1024]{0,1:T(8,128)} async-done(((f32[48,4096]{0,1:T(8,128)}), f32[48,1024]{0,1:T(8,128)}) %reduce-scatter.2.cloned.1.call-update) | async-done | bytes 196624 | tf_op jit(solution)/shard_map/reduce_scatter | solution.py:185
  549.4 1.1 copy.268
  551.2 0.7 slice.122
  551.9 332.1 %all-reduce.11.cloned.1.call-done = f32[48,1024]{0,1:T(8,128)} async-done(((f32[48,1024]{0,1:T(8,128)}), f32[48,1024]{0,1:T(8,128)}) %all-reduce.11.cloned.1.call-update) | async-done | bytes 196624 | tf_op jit(solution)/shard_map/psum | solution.py:186
  884.0 1.9 copy.248
  885.9 56.3 %all-reduce.9.cloned.1.call-done = f32[12,8192]{1,0:T(8,128)} async-done(((f32[12,8192]{1,0:T(8,128)}), f32[12,8192]{1,0:T(8,128)}) %all-reduce.9.cloned.1.call-update) | async-done | bytes 393232 | tf_op jit(solution)/shard_map/psum | solution.py:184
  942.2 1.9 copy.344
  (265 shorter events, 25.9 us)
Async XLA Ops:
  7.2 1.4 copy-start
  10.2 70.0 %all-to-all-start = ((bf16[6,128,128]{2,0,1:T(8,128)(2,1)}), bf16[6,128,128]{2,0,1:T(8,128)(2,1)S(1)}, u32[]{:S(2)}, u32[]{:S(2)}) async-start(bf16[6,128,128]{2,0,1:T(8,128)(2,1)} %select_bitcast_fusion.3), calls=%async_computation | async-start | bytes 524288 | tf_op jit(solution)/shard_map/all_to_all | solution.py:121
  76.6 1.0 copy-start.2
  80.2 16.4 %copy-start.6 = (s32[1,8,4]{1,2,0:T(4,128)S(1)}, s32[1,8,4]{1,2,0:T(4,128)}, u32[]{:S(2)}) copy-start(s32[1,8,4]{1,2,0:T(4,128)} %param.15) | copy-start | bytes 388
  80.2 16.6 %copy-start.3 = (f32[1,3,2048]{2,0,1:T(1,128)S(1)}, f32[1,3,2048]{2,0,1:T(1,128)}, u32[]{:S(2)}) copy-start(f32[1,3,2048]{2,0,1:T(1,128)} %param.16) | copy-start | bytes 73732
  80.2 16.8 %copy-start.4 = (s32[1,3,2048]{2,0,1:T(1,128)S(1)}, s32[1,3,2048]{2,0,1:T(1,128)}, u32[]{:S(2)}) copy-start(s32[1,3,2048]{2,0,1:T(1,128)} %param.17) | copy-start | bytes 73732
  80.2 17.7 %copy-start.1 = (bf16[6,128,128]{2,0,1:T(8,128)(2,1)}, bf16[6,128,128]{2,0,1:T(8,128)(2,1)S(1)}, u32[]{:S(2)}) copy-start(bf16[6,128,128]{2,0,1:T(8,128)(2,1)S(1)} %all-to-all-done) | copy-start | bytes 589828
  80.2 91.3 %all-to-all-start.1 = ((bf16[48,128,128]{2,0,1:T(8,128)(2,1)}), bf16[48,128,128]{2,0,1:T(8,128)(2,1)S(1)}, u32[]{:S(2)}, u32[]{:S(2)}) async-start(bf16[48,128,128]{2,0,1:T(8,128)(2,1)} %select_bitcast_fusion), calls=%async_computation.1 | async-start | bytes 3145728 | tf_op jit(solution)/shard_map/all_to_all | solution.py:122
  96.4 452.8 %reduce-scatter.2.cloned.1.call-start = ((), (), s32[]{:S(2)}) async-start(), calls=%async_computation.5 | async-start | bytes 2621440 | tf_op jit(solution)/shard_map/reduce_scatter | solution.py:185
  99.6 73.7 %copy-start.5 = (f32[4,2,3,256]{3,1,0,2:T(2,128)S(1)}, f32[4,2,3,256]{3,1,0,2:T(2,128)}, u32[]{:S(2)}) copy-start(f32[4,2,3,256]{3,1,0,2:T(2,128)} %custom-call.11) | copy-start | bytes 73732
  292.1 171.7 %copy-start.7 = (s32[1,1,128]{2,1,0:T(1,128)S(1)}, s32[1,1,128]{2,1,0:T(1,128)}, u32[]{:S(2)}) copy-start(s32[1,1,128]{2,1,0:T(1,128)} %param.14) | copy-start | bytes 1540
  514.1 369.9 %all-reduce.11.cloned.1.call-start = ((), (), s32[]{:S(2)}) async-start(), calls=%async_computation.6 | async-start | bytes 1048576 | tf_op jit(solution)/shard_map/psum | solution.py:186
  549.3 392.9 %all-reduce.9.cloned.1.call-start = ((), (), s32[]{:S(2)}) async-start(), calls=%async_computation.4 | async-start | bytes 1048576 | tf_op jit(solution)/shard_map/psum | solution.py:184
Sparse Core Ops, SparseCore 0:
  514.2 34.9 reduce-scatter.1
  553.1 330.8 all-reduce.10
  886.9 55.2 all-reduce.8
where the time goes:
time: 952 us; the launch traced here: 951 us
  waiting for transfers between devices  495 us (52%)
  blocking collectives  187 us (20%)
  other arithmetic  108 us (11%)
  local copies, waits for them, and re-layouts  69 us (7%)
  matrix products  40.4 us (4%)
  starting transfers between devices  35.9 us (4%)
  between operations  14.2 us (1%)
    psum x1, waiting for transfers between devices, on_device(): code_grad = lax.psum(codeword_portion, 'space')  332 us
    all_to_all x1, blocking collectives, on_device(): lax.all_to_all(slot_grads, 'space', split_axis=1, concat_axis=1, tiled=True)  172 us
    all_to_all x1, waiting for transfers between devices, on_device(): lax.all_to_all(palette_out, 'space', split_axis=1, concat_axis=1, tiled=T...  71.7 us
    psum x1, waiting for transfers between devices, on_device(): resid_grad = lax.psum(resid_part, 'code')  56.3 us
    scatter-add x1, other arithmetic, on_device(): jax.ops.segment_sum(palette_owned.T, word_ids, num_segments=WORDS)  45.7 us
    reduce_scatter x1, waiting for transfers between devices, on_device(): lax.psum_scatter(word_term, 'code', scatter_dimension=1, tiled=True)  35.1 us
    dot_general x12, matrix products, composite(): mixed = jnp.dot(weight, palette.T, precision=lax.Precision.HIGHEST)  33.9 us
    gather x2, local copies, waits for them, and re-layouts, decode(): looked = jnp.take(codebook, word_ids, axis=1).astype(jnp.float32)  28.8 us
  transfers between devices with their start and end apart: 5, of which 4 were waited for; matrix products, arithmetic and copies ran while one was open for 4% of the time, Pallas kernels for 0%

commit v1 on v0

--- a/solution.py
+++ b/solution.py
@@ -183,7 +183,8 @@
     foot_grad = owned[:GEO]
     resid_grad = lax.psum(resid_part, "code")
     codeword_portion = lax.psum_scatter(word_term, "code", scatter_dimension=1, tiled=True)
-    code_grad = lax.psum(codeword_portion, "space")
+    parts = lax.all_gather(codeword_portion, "space", axis=0, tiled=False)
+    code_grad = parts.sum(axis=0)
     rendered = (
         images.reshape(tiles_here, 3, TILE_PIX)
         .transpose(1, 0, 2)

time: 952 us -> 786 us (0.83)
  waiting for transfers between devices: 495 us -> 325 us
    psum x1 -> x0, waiting for transfers between devices: 332 us -> none  [on_device(): code_grad = lax.psum(codeword_portion, 'space')]
    all_gather x0 -> x1, waiting for transfers between devices: none -> 171 us  [on_device(): parts = lax.all_gather(codeword_portion, 'space', axis=0, tiled=False)]
    reduce_sum x0 -> x1, other arithmetic: none -> 9.86 us  [on_device(): code_grad = parts.sum(axis=0)]
  transfers between devices with their start and end apart: 5 -> 5, of which waited for: 4 -> 4; matrix products, arithmetic and copies ran while one was open for 4% -> 6% of each run, Pallas kernels for 0% -> 0%
where the time goes in v1:
time: 786 us; the launch traced here: 785 us
  waiting for transfers between devices  325 us (41%)
  blocking collectives  187 us (24%)
  other arithmetic  117 us (15%)
  local copies, waits for them, and re-layouts  64.4 us (8%)
  matrix products  39.7 us (5%)
  starting transfers between devices  35.9 us (5%)
  between operations  14.2 us (2%)
    all_to_all x1, blocking collectives, on_device(): lax.all_to_all(slot_grads, 'space', split_axis=1, concat_axis=1, tiled=True)  172 us
    all_gather x1, waiting for transfers between devices, on_device(): parts = lax.all_gather(codeword_portion, 'space', axis=0, tiled=False)  171 us
    all_to_all x1, waiting for transfers between devices, on_device(): lax.all_to_all(palette_out, 'space', split_axis=1, concat_axis=1, tiled=T...  71.7 us
    psum x1, waiting for transfers between devices, on_device(): resid_grad = lax.psum(resid_part, 'code')  47.8 us
    scatter-add x1, other arithmetic, on_device(): jax.ops.segment_sum(palette_owned.T, word_ids, num_segments=WORDS)  45.7 us
    reduce_scatter x1, waiting for transfers between devices, on_device(): lax.psum_scatter(word_term, 'code', scatter_dimension=1, tiled=True)  35.1 us
    dot_general x12, matrix products, composite(): mixed = jnp.dot(weight, palette.T, precision=lax.Precision.HIGHEST)  33.9 us
    another operation x21, other arithmetic  25.8 us
  transfers between devices with their start and end apart: 5, of which 4 were waited for; matrix products, arithmetic and copies ran while one was open for 6% of the time, Pallas kernels for 0%

profile of v1, /device:TPU:8, one launch (start us, length us, event | category | flops | bytes accessed | tf_op | source)
XLA Modules:
  0.0 784.8 jit_solution(4442039401856066829)
XLA Ops:
  7.2 0.7 compare_and_fusion.1
  8.5 0.7 gather_fusion
  9.2 0.9 select_bitcast_fusion.3
  10.2 19.5 %all-to-all-start = ((bf16[6,128,128]{2,0,1:T(8,128)(2,1)}), bf16[6,128,128]{2,0,1:T(8,128)(2,1)S(1)}, u32[]{:S(2)}, u32[]{:S(2)}) async-start(bf16[6,128,128]{2,0,1:T(8,128)(2,1)} %select_bitcast_fusion.3), calls=%async_computation | async-start | bytes 524288 | tf_op jit(solution)/shard_map/all_to_all | solution.py:121
  29.7 0.8 compare_and_fusion
  30.4 0.8 fusion.63
  31.2 1.1 copy.229
  32.3 14.9 %all_gather.9 = bf16[48,4096]{0,1:T(8,128)(2,1)S(1)} all-gather(bf16[48,1024]{0,1:T(8,128)(2,1)S(1)} %copy.229), channel_id=1, replica_groups=mesh['space'=128,'code'=4] {'code'}, dimensions={1}, use_global_device_ids=true | all-gather | bytes 491520 | tf_op jit(solution)/shard_map/all_gather | solution.py:115
  47.2 24.0 %gather_fusion.2 = bf16[8192,48]{1,0:T(8,128)(2,1)S(1)} fusion(bf16[48,4096]{0,1:T(8,128)(2,1)S(1)} %all_gather.9, s32[8192]{0:T(1024)S(1)} %fusion.63), kind=kCustom, calls=%fused_computation.2 | custom fusion | bytes 1605632 | tf_op jit(solution)/shard_map/jit(_take)/gather | solution.py:104
  71.2 0.8 copy.230
  73.4 0.9 gather_fusion.3
  74.3 1.4 select_bitcast_fusion
  75.7 16.2 %all-to-all-start.1 = ((bf16[48,128,128]{2,0,1:T(8,128)(2,1)}), bf16[48,128,128]{2,0,1:T(8,128)(2,1)S(1)}, u32[]{:S(2)}, u32[]{:S(2)}) async-start(bf16[48,128,128]{2,0,1:T(8,128)(2,1)} %select_bitcast_fusion), calls=%async_computation.1 | async-start | bytes 3145728 | tf_op jit(solution)/shard_map/all_to_all | solution.py:122
  93.6 1.5 gather_fusion.1
  95.2 71.7 %all-to-all-done.1 = bf16[48,128,128]{2,0,1:T(8,128)(2,1)S(1)} async-done(((bf16[48,128,128]{2,0,1:T(8,128)(2,1)}), bf16[48,128,128]{2,0,1:T(8,128)(2,1)S(1)}, u32[]{:S(2)}, u32[]{:S(2)}) %all-to-all-start.1) | async-done | bytes 1572896 | tf_op jit(solution)/shard_map/all_to_all | solution.py:122
  168.0 0.9 copy.255
  168.9 107.4 %while.16 = (s32[]{:T(128)}, f32[4,2,3,256]{3,1,0,2:T(2,128)}, f32[4,2,6,512]{3,2,1,0:T(8,128)S(1)}, f32[4,2,48,512]{3,2,1,0:T(8,128)}, bf16[4,2,6,512]{3,1,0,2:...) while((s32[]{:T(128)}, f32[4,2,3,256]{3,1,0,2:T(2,128)}, ...), condition=%wide.region_14.15_spmd.clone.clone, body=%wide.region_1.14_spmd.clone.clone.sunk | while | flops 552732160 | bytes 30296212 | solution.py:152
  169.9 1.9 fusion.93
  171.9 2.6 multiply_reduce_fusion.7
  175.5 2.6 fusion.94
  178.2 0.7 fusion.95
  179.5 2.4 fusion.98
  182.0 3.5 multiply_multiply_fusion.3
  186.4 4.3 fusion.96
  192.0 3.5 fusion.97
  196.7 1.9 fusion.93
  198.7 2.6 multiply_reduce_fusion.7
  202.3 2.5 fusion.94
  205.0 0.7 fusion.95
  206.3 2.4 fusion.98
  208.8 3.5 multiply_multiply_fusion.3
  213.2 4.3 fusion.96
  218.8 3.5 fusion.97
  223.5 1.9 fusion.93
  225.4 2.6 multiply_reduce_fusion.7
  229.1 2.6 fusion.94
  231.8 0.7 fusion.95
  233.1 2.4 fusion.98
  235.6 3.5 multiply_multiply_fusion.3
  240.0 4.3 fusion.96
  245.6 3.5 fusion.97
  250.3 1.9 fusion.93
  252.2 2.6 multiply_reduce_fusion.7
  255.8 2.6 fusion.94
  258.6 0.7 fusion.95
  259.9 2.5 fusion.98
  262.4 3.5 multiply_multiply_fusion.3
  266.8 4.3 fusion.96
  272.4 3.5 fusion.97
  276.2 2.3 concatenate.15
  279.2 4.1 convolution_bitcast_fusion.1
  283.3 3.2 copy.242
  286.5 171.7 %all_to_all.15 = f32[54,128,128]{2,0,1:T(8,128)S(1)} all-to-all(f32[54,128,128]{2,0,1:T(8,128)} %copy.242), channel_id=1, replica_groups=mesh['space'=128,'code'=4] {'space'}, dimensions={1} | all-to-all | bytes 7077888 | tf_op jit(solution)/shard_map/all_to_all | solution.py:176
  458.2 1.7 fusion.53
  460.1 2.7 copy.257
  462.8 45.7 %scatter_custom_fusion = f32[4096,48]{1,0:T(8,128)} fusion(s32[8192]{0:T(1024)} %param.12, f32[8192,48]{1,0:T(8,128)} %bitcast.187, f32[]{:T(128)} %constant.114.clone.1), kind=kCustom, calls=%fused_computation.109 | custom fusion | flops 393216 | bytes 786944 | tf_op jit(solution)/shard_map/scatter-add | solution.py:181
  508.5 35.1 %reduce-scatter.2.cloned.1.call-done = f32[48,1024]{0,1:T(8,128)} async-done(((f32[48,4096]{0,1:T(8,128)}), f32[48,1024]{0,1:T(8,128)}) %reduce-scatter.2.cloned.1.call-update) | async-done | bytes 196624 | tf_op jit(solution)/shard_map/reduce_scatter | solution.py:185
  543.6 1.9 copy.245
  545.7 1.1 copy.268
  547.5 0.7 slice.122
  548.2 170.6 %all-gather.3.cloned.1.call-done = f32[6144,1024]{1,0:T(8,128)} async-done(((f32[48,1024]{1,0:T(8,128)}), f32[6144,1024]{1,0:T(8,128)}) %all-gather.3.cloned.1.call-update) | async-done | bytes 25165840 | tf_op jit(solution)/shard_map/all_gather | solution.py:186
  718.7 9.9 %reduce_sum.90 = f32[48,1024]{1,0:T(8,128)} reduce(f32[128,48,1024]{2,1,0:T(8,128)} %bitcast.182, f32[]{:T(128)} %constant.114.clone.1), dimensions={0}, to_apply=%region_18.19 | reduce | flops 6242304 | bytes 25362436 | tf_op jit(solution)/shard_map/reduce_sum | solution.py:187
  728.6 47.8 %all-reduce.8.cloned.1.call-done = f32[12,8192]{1,0:T(8,128)} async-done(((f32[12,8192]{1,0:T(8,128)}), f32[12,8192]{1,0:T(8,128)}) %all-reduce.8.cloned.1.call-update) | async-done | bytes 393232 | tf_op jit(solution)/shard_map/psum | solution.py:184
  776.4 1.9 copy.343
  (268 shorter events, 26.5 us)
Async XLA Ops:
  7.2 1.4 copy-start
  10.2 65.5 %all-to-all-start = ((bf16[6,128,128]{2,0,1:T(8,128)(2,1)}), bf16[6,128,128]{2,0,1:T(8,128)(2,1)S(1)}, u32[]{:S(2)}, u32[]{:S(2)}) async-start(bf16[6,128,128]{2,0,1:T(8,128)(2,1)} %select_bitcast_fusion.3), calls=%async_computation | async-start | bytes 524288 | tf_op jit(solution)/shard_map/all_to_all | solution.py:121
  72.0 1.0 copy-start.3
  75.6 16.4 %copy-start.7 = (s32[1,8,4]{1,2,0:T(4,128)S(1)}, s32[1,8,4]{1,2,0:T(4,128)}, u32[]{:S(2)}) copy-start(s32[1,8,4]{1,2,0:T(4,128)} %param.15) | copy-start | bytes 388
  75.7 16.6 %copy-start.4 = (f32[1,3,2048]{2,0,1:T(1,128)S(1)}, f32[1,3,2048]{2,0,1:T(1,128)}, u32[]{:S(2)}) copy-start(f32[1,3,2048]{2,0,1:T(1,128)} %param.16) | copy-start | bytes 73732
  75.7 16.8 %copy-start.5 = (s32[1,3,2048]{2,0,1:T(1,128)S(1)}, s32[1,3,2048]{2,0,1:T(1,128)}, u32[]{:S(2)}) copy-start(s32[1,3,2048]{2,0,1:T(1,128)} %param.17) | copy-start | bytes 73732
  75.7 17.7 %copy-start.2 = (bf16[6,128,128]{2,0,1:T(8,128)(2,1)}, bf16[6,128,128]{2,0,1:T(8,128)(2,1)S(1)}, u32[]{:S(2)}) copy-start(bf16[6,128,128]{2,0,1:T(8,128)(2,1)S(1)} %all-to-all-done) | copy-start | bytes 589828
  75.7 91.3 %all-to-all-start.1 = ((bf16[48,128,128]{2,0,1:T(8,128)(2,1)}), bf16[48,128,128]{2,0,1:T(8,128)(2,1)S(1)}, u32[]{:S(2)}, u32[]{:S(2)}) async-start(bf16[48,128,128]{2,0,1:T(8,128)(2,1)} %select_bitcast_fusion), calls=%async_computation.1 | async-start | bytes 3145728 | tf_op jit(solution)/shard_map/all_to_all | solution.py:122
  91.9 451.7 %reduce-scatter.2.cloned.1.call-start = ((), (), s32[]{:S(2)}) async-start(), calls=%async_computation.5 | async-start | bytes 2621440 | tf_op jit(solution)/shard_map/reduce_scatter | solution.py:185
  286.5 171.7 %copy-start.8 = (s32[1,1,128]{2,1,0:T(1,128)S(1)}, s32[1,1,128]{2,1,0:T(1,128)}, u32[]{:S(2)}) copy-start(s32[1,1,128]{2,1,0:T(1,128)} %param.14) | copy-start | bytes 1540
  508.5 38.3 %copy-start.6 = (f32[4,2,3,256]{3,1,0,2:T(2,128)S(1)}, f32[4,2,3,256]{3,1,0,2:T(2,128)}, u32[]{:S(2)}) copy-start(f32[4,2,3,256]{3,1,0,2:T(2,128)} %get-tuple-element.64) | copy-start | bytes 73732
  508.5 210.2 %all-gather.3.cloned.1.call-start = ((), (), s32[]{:S(2)}) async-start(), calls=%async_computation.6 | async-start | bytes 25362432 | tf_op jit(solution)/shard_map/all_gather | solution.py:186
  545.5 230.9 %all-reduce.8.cloned.1.call-start = ((), (), s32[]{:S(2)}) async-start(), calls=%async_computation.4 | async-start | bytes 1048576 | tf_op jit(solution)/shard_map/psum | solution.py:184
  718.7 59.5 %copy-start.1 = (bf16[1,6,8192]{2,1,0:T(8,128)(2,1)S(1)}, bf16[1,6,8192]{2,1,0:T(8,128)(2,1)}, u32[]{:S(2)}) copy-start(bf16[1,6,8192]{2,1,0:T(8,128)(2,1)} %param.10) | copy-start | bytes 294916
Sparse Core Ops, SparseCore 0:
  508.6 34.9 reduce-scatter.1
  547.8 170.8 all-gather.2
  721.8 54.5 all-reduce.7
